TPU v7x, 512 devices: a whole 4x4x16 slice. The times are simulated.
512 devices in a mesh: segment: 2 (over z_hi), group: 32 (over y, x, core), tensor: 8 (over z_lo).
Axes of the slice: x: 4, y: 4, z: 16 (z_hi: 2, z_lo: 8; z = z_hi * 8 + z_lo), core: 2. Of those that a mesh axis runs over, the one named last changes fastest.
Arguments:
- hidden: bfloat16 [24576, 8192], P(('segment', 'group'), 'tensor'), may hold values from -6 to 6
- prompt_queries: bfloat16 [24576, 8192], P(('segment', 'group'), 'tensor'), may hold values from -6 to 6
- prompt_key_values: bfloat16 [24576, 2048], P(('segment', 'group'), 'tensor'), may hold values from -6 to 6
- adapter_down_weight: bfloat16 [3, 8192, 128], P(None, 'tensor'), may hold values from -0.0625 to 0.0625
- adapter_up_weight: bfloat16 [3, 128, 2048], P(None, None, 'tensor'), may hold values from -0.5 to 0.5
- adapter_ranks: int32 [3], replicated, may hold values from 8 to 128, as said below
- tenant: int32 [64, 16], P(('segment', 'group')), may hold values from 0 to 2
- lengths: int32 [64, 16], replicated, may hold values from 1 to 32, 384 in all within a row
- owner: int32 [64, 16], replicated, may hold values from 0 to 31, as said below
- cached_key_values: bfloat16 [1024, 256, 2048], P(('segment', 'group'), 'tensor'), may hold values from -6 to 6
- draft_queries: bfloat16 [4096, 8192], P(('segment', 'group'), 'tensor'), may hold values from -6 to 6
- draft_key_values: bfloat16 [4096, 2048], P(('segment', 'group'), 'tensor'), may hold values from -6 to 6
Outputs:
- prompt_out: bfloat16 [24576, 8192], P(('segment', 'group'), 'tensor')
- decode_out: bfloat16 [4096, 8192], P(('segment', 'group'), 'tensor')
Inputs may be any that keep to these rules, and one draw needn't show every extreme that they name: `owner`: each decode group receives exactly one request of each index i < 16 from the other section; one prefill group sends exactly 1 request to each of 16 decode groups and none to the others. `adapter_ranks`: powers of two.
All inputs are finite; a program needn't handle non-finite values.
Results may differ from a plain program's by a relative error of at most 0.0083.
Values may be sent and summed in bfloat16 or wider, within the bound.
A program may use at most 128 MiB of HBM per device.

v0:
```python
import jax
import jax.numpy as jnp
from jax import lax
from jax.sharding import PartitionSpec as P

HEAD_SIZE = 128
SPEC = 4
GQA = 8
MAXLEN = 32


negative = -1e30


def from_partner(block, axis, stride):
    count = lax.axis_size(axis)
    route = []
    for low in range(count):
        high = low | 1 << stride
        if high != low and high < count:
            route += [(low, high), (high, low)]
    return lax.ppermute(block, axis, route)


def combined_all(shard, axis, combine):
    everything = jax.tree.map(lambda part: lax.all_gather(part, axis), shard)
    leading = jax.tree.map(lambda part: part[0], everything)

    def turn(k, so_far):
        return combine(so_far, jax.tree.map(lambda part: part[k], everything))

    return lax.fori_loop(1, lax.axis_size(axis), turn, leading)


def pack_slots(key_value_rows, row_lengths, row_owner, groups, capacity):
    requests = row_lengths.shape[0]
    req_ends = jnp.cumsum(row_lengths)
    req_starts = req_ends - row_lengths
    req_order = jnp.arange(requests, dtype=jnp.int32)
    before = (req_order[None, :] < req_order[:, None]) & (row_owner[None, :] == row_owner[:, None])
    slot_place = row_owner * capacity + jnp.sum(before.astype(jnp.int32), axis=1)
    slot_ids = jnp.arange(groups * capacity, dtype=jnp.int32)
    slot_hit = slot_ids[:, None] == slot_place[None, :]
    slot_start = jnp.sum(jnp.where(slot_hit, req_starts[None, :], 0), axis=1)
    slot_length = jnp.sum(jnp.where(slot_hit, row_lengths[None, :], 0), axis=1)
    offsets = jnp.arange(MAXLEN, dtype=jnp.int32)
    is_live = offsets[None, :] < slot_length[:, None]
    row_index = jnp.where(is_live, slot_start[:, None] + offsets[None, :], 0)
    packed = jnp.where(
        is_live[:, :, None], key_value_rows[row_index], jnp.zeros((), key_value_rows.dtype)
    )
    return packed.reshape(groups, capacity, MAXLEN, key_value_rows.shape[1])


def attend_parts(queries, key_vals, is_live):
    scores = jnp.einsum(
        "rsjgd,rljd->rsjgl", queries, key_vals[:, :, :, 0], preferred_element_type=jnp.float32
    ) * HEAD_SIZE ** (-0.5)
    key_mask = is_live[:, :, None, None, :]
    scores = jnp.where(key_mask, scores, negative)
    row_max = jnp.max(scores, axis=-1)
    exp_scores = jnp.where(key_mask, jnp.exp(scores - row_max[..., None]), 0.0)
    exp_total = jnp.sum(exp_scores, axis=-1)
    numerator = jnp.einsum(
        "rsjgl,rljd->rsjgd",
        exp_scores,
        key_vals[:, :, :, 1].astype(jnp.float32),
        precision=lax.Precision.HIGHEST,
    )
    return (row_max, exp_total, numerator)


def combine_parts(first_part, second_part):
    max_one, total_one, numer_one = first_part
    max_two, total_two, numer_two = second_part
    joint_max = jnp.maximum(max_one, max_two)
    factor_one = jnp.exp(max_one - joint_max)
    factor_two = jnp.exp(max_two - joint_max)
    return (
        joint_max,
        total_one * factor_one + total_two * factor_two,
        numer_one * factor_one[..., None] + numer_two * factor_two[..., None],
    )


def body(
    hidden,
    prompt_queries,
    prompt_key_values,
    adapter_down_weight,
    adapter_up_weight,
    adapter_ranks,
    tenant,
    lengths,
    owner,
    cached_key_values,
    draft_queries,
    draft_key_values,
):
    groups = lax.axis_size("group")
    segment_idx = lax.axis_index("segment")
    group_idx = lax.axis_index("group")
    tensor_idx = lax.axis_index("tensor")
    here_row = segment_idx * groups + group_idx
    tokens = hidden.shape[0]
    requests = tenant.shape[1]
    capacity = max(1, requests // groups)
    adapter_list = adapter_down_weight.shape[0]
    local_width = prompt_key_values.shape[1]
    local_kv = local_width // (2 * HEAD_SIZE)
    my_lengths = lax.dynamic_index_in_dim(lengths, here_row, 0, keepdims=False)
    req_ends = jnp.cumsum(my_lengths)
    positions = jnp.arange(tokens, dtype=jnp.int32)
    request = jnp.sum((positions[:, None] >= req_ends[None, :]).astype(jnp.int32), axis=1)
    pick_request = request[:, None] == jnp.arange(requests, dtype=jnp.int32)[None, :]
    tenant_adapter = jnp.sum(jnp.where(pick_request, tenant[0][None, :], 0), axis=1)
    select_adapter = (
        tenant_adapter[None, :] == jnp.arange(adapter_list, dtype=jnp.int32)[:, None]
    )[:, :, None]
    rank_tok = jnp.sum(jnp.where(select_adapter[:, :, 0], adapter_ranks[:, None], 0), axis=0)
    partial_value_sum = jnp.einsum(
        "lm,omt->olt", hidden, adapter_down_weight, preferred_element_type=jnp.float32
    )
    selected = jnp.sum(jnp.where(select_adapter, partial_value_sum, 0.0), axis=0)
    summed = lax.psum(selected, "tensor")
    columns = jnp.arange(summed.shape[1], dtype=jnp.int32)
    reduced_rows = jnp.where(columns[None, :] < rank_tok[:, None], summed, 0.0).astype(jnp.bfloat16)
    expanded_rows = jnp.einsum(
        "ot,uth->uoh", reduced_rows, adapter_up_weight, preferred_element_type=jnp.float32
    )
    adapter_delta = jnp.sum(jnp.where(select_adapter, expanded_rows, 0.0), axis=0)
    lowrank_factor = 8.0 / jnp.sqrt(rank_tok.astype(jnp.float32))
    key_value_rows = (
        prompt_key_values.astype(jnp.float32) + lowrank_factor[:, None] * adapter_delta
    ).astype(jnp.bfloat16)
    kv_split = key_value_rows.reshape(tokens, local_kv, 2, HEAD_SIZE)
    queries = prompt_queries.reshape(tokens, local_kv, GQA, HEAD_SIZE)
    scores = jnp.einsum(
        "pjgd,kjd->jgpk", queries, kv_split[:, :, 0], preferred_element_type=jnp.float32
    ) * HEAD_SIZE ** (-0.5)
    allowed = (request[:, None] == request[None, :]) & (positions[None, :] <= positions[:, None])
    scores = jnp.where(allowed, scores, negative)
    row_max = jnp.max(scores, axis=-1, keepdims=True)
    exp_scores = jnp.exp(scores - row_max)
    weights = (exp_scores / jnp.sum(exp_scores, axis=-1, keepdims=True)).astype(jnp.bfloat16)
    attended = jnp.einsum(
        "jgpk,kjd->pjgd", weights, kv_split[:, :, 1], preferred_element_type=jnp.float32
    )
    prompt_out = attended.reshape(tokens, local_kv * GQA * HEAD_SIZE).astype(jnp.bfloat16)
    packed = pack_slots(
        key_value_rows,
        my_lengths,
        lax.dynamic_index_in_dim(owner, here_row, 0, keepdims=False),
        groups,
        capacity,
    )
    crossed = from_partner(packed, "segment", 0)
    routed = lax.all_to_all(crossed, "group", split_axis=0, concat_axis=0, tiled=True)
    other_rows = (1 - segment_idx) * groups
    src_owner = lax.dynamic_slice_in_dim(owner, other_rows, groups, 0)
    src_lengths = lax.dynamic_slice_in_dim(lengths, other_rows, groups, 0)
    is_mine = src_owner == group_idx
    source = jnp.sum(jnp.where(is_mine, jnp.arange(groups, dtype=jnp.int32)[:, None], 0), axis=0)
    pick_source = source[:, None] == jnp.arange(groups, dtype=jnp.int32)[None, :]
    mine_rows = jnp.any(pick_source[:, :, None] & is_mine[None, :, :], axis=1)
    req_order = jnp.arange(requests, dtype=jnp.int32)
    slot_in = jnp.sum(
        (mine_rows & (req_order[None, :] < req_order[:, None])).astype(jnp.int32), axis=1
    )
    src_length = jnp.sum(jnp.where(pick_source, src_lengths.T, 0), axis=1)
    handed = routed.reshape(groups * capacity, MAXLEN, local_width)[source * capacity + slot_in]
    draft_ids = jnp.arange(SPEC, dtype=jnp.int32)
    own_live = draft_ids[None, :] <= draft_ids[:, None]
    spread = lax.all_to_all(handed, "tensor", split_axis=1, concat_axis=2, tiled=True)
    piece = spread.shape[1]
    new_pos = tensor_idx * piece + jnp.arange(piece, dtype=jnp.int32)
    live_new = new_pos[None, :] < src_length[:, None]
    all_q, all_own = (
        lax.all_gather(draft_queries, "tensor", axis=1, tiled=True),
        lax.all_gather(draft_key_values, "tensor", axis=1, tiled=True),
    )
    full_width = all_own.shape[1]
    key_vals = jnp.concatenate(
        [cached_key_values, spread, all_own.reshape(requests, SPEC, full_width)], axis=1
    )
    key_vals = key_vals.reshape(
        requests, key_vals.shape[1], full_width // (2 * HEAD_SIZE), 2, HEAD_SIZE
    )
    is_live = jnp.concatenate(
        [
            jnp.ones((requests, SPEC, cached_key_values.shape[1]), bool),
            jnp.broadcast_to(live_new[:, None, :], (requests, SPEC, piece)),
            jnp.broadcast_to(own_live[None] & (tensor_idx == 0), (requests, SPEC, SPEC)),
        ],
        axis=2,
    )
    all_queries = all_q.reshape(requests, SPEC, full_width // (2 * HEAD_SIZE), GQA, HEAD_SIZE)
    parts = attend_parts(all_queries, key_vals, is_live)
    joint_max, joint_total, joint_numer = combined_all(parts, "tensor", combine_parts)
    result = (joint_numer / joint_total[..., None]).reshape(requests * SPEC, all_q.shape[1])
    out_width = draft_queries.shape[1]
    decode_out = lax.dynamic_slice_in_dim(result, tensor_idx * out_width, out_width, 1).astype(
        jnp.bfloat16
    )
    return (prompt_out, decode_out)


def solution(mesh):
    return jax.shard_map(
        body,
        mesh=mesh,
        in_specs=(
            P(("segment", "group"), "tensor"),
            P(("segment", "group"), "tensor"),
            P(("segment", "group"), "tensor"),
            P(None, "tensor", None),
            P(None, None, "tensor"),
            P(),
            P(("segment", "group"), None),
            P(),
            P(),
            P(("segment", "group"), "tensor", None),
            P(("segment", "group"), "tensor"),
            P(("segment", "group"), "tensor"),
        ),
        out_specs=(P(("segment", "group"), "tensor"), P(("segment", "group"), "tensor")),
        check_vma=False,
    )
```

profile of v0, /device:TPU:6, one launch (start us, length us, event | category | flops | bytes accessed | tf_op | source)
XLA Modules:
  0.0 674.7 jit_solution(2389543172784825067)
XLA Ops:
  12.6 70.0 %all-reduce.1 = bf16[384,128]{0,1:T(8,128)(2,1)S(1)} all-reduce(f32[384,128]{0,1:T(8,128)S(1)} %bitcast.161), channel_id=1, replica_groups=mesh['segment'=2,'group'=32,'tensor'=8] {'tensor'}, use_global_device_ids=true, to_apply=%region_5.6 | all-reduce | flops 49152 | bytes 294912 | tf_op jit(solution)/shard_map/psum | solution.py:125
  83.2 3.9 gather_fusion
  88.2 25.5 %collective-permute-start = (bf16[32,1,32,256]{3,2,1,0:T(8,128)(2,1)}, bf16[32,1,32,256]{3,2,1,0:T(8,128)(2,1)}, u32[]{:S(2)}, u32[]{:S(2)}) collective-permute-start(bf16[32,1,32,256]{3,2,1,0:T(8,128)(2,1)} %broadcast_select_fusion), channel_id=1, source_target_pairs={{0,256},{256,0},{1,257},{257,1},{2,258},{258,2},{3,259},{259,3},{4... | collective-permute-start | bytes 1572872 | tf_op jit(solution)/shard_map/ppermute | solution.py:22
  114.0 15.9 %collective-permute-done = bf16[32,1,32,256]{3,2,1,0:T(8,128)(2,1)} collective-permute-done((bf16[32,1,32,256]{3,2,1,0:T(8,128)(2,1)}, bf16[32,1,32,256]{3,2,1,0:T(8,128)(2,1)}, u32[]{:S(2)}, u32[]{:S(2)}) %collective-permute-start) | collective-permute-done | bytes 524320 | tf_op jit(solution)/shard_map/ppermute | solution.py:22
  129.9 7.6 %all-to-all-start = ((bf16[32,1,32,256]{3,2,1,0:T(8,128)(2,1)}), bf16[32,1,32,256]{3,2,1,0:T(8,128)(2,1)}, u32[]{:S(2)}, u32[]{:S(2)}) async-start(bf16[32,1,32,256]{3,2,1,0:T(8,128)(2,1)} %collective-permute-done), calls=%async_computation | async-start | bytes 1048576 | tf_op jit(solution)/shard_map/all_to_all | solution.py:158
  138.0 8.9 %all-to-all-done = bf16[32,1,32,256]{3,2,1,0:T(8,128)(2,1)} async-done(((bf16[32,1,32,256]{3,2,1,0:T(8,128)(2,1)}), bf16[32,1,32,256]{3,2,1,0:T(8,128)(2,1)}, u32[]{:S(2)}, u32[]{:S(2)}) %all-to-all-start) | async-done | bytes 524320 | tf_op jit(solution)/shard_map/all_to_all | solution.py:158
  149.4 4.0 all-to-all-start.1
  153.5 2.7 concatenate.14
  158.4 47.5 %all_gather.24 = bf16[64,2048]{1,0:T(8,128)(2,1)S(1)} all-gather(bf16[64,256]{1,0:T(8,128)(2,1)S(1)} %copy-done.5), channel_id=1, replica_groups=mesh['segment'=2,'group'=32,'tensor'=8] {'tensor'}, dimensions={1}, use_global_device_ids=true | all-gather | bytes 294912 | tf_op jit(solution)/shard_map/all_gather | solution.py:180
  208.4 2.5 copy.169
  214.3 2.2 convolution_bitcast_fusion
  220.5 2.5 fusion.10
  223.0 2.3 copy.154
  227.5 88.9 %all-gather.1 = f32[128,4,8,8]{3,2,1,0:T(8,128)S(1)} all-gather(f32[16,4,8,8]{3,2,1,0:T(8,128)S(1)} %copy.145), channel_id=3, replica_groups=mesh['segment'=2,'group'=32,'tensor'=8] {'tensor'}, dimensions={0}, use_global_device_ids=true | all-gather | bytes 147456 | tf_op jit(solution)/shard_map/all_gather | solution.py:26
  319.1 87.9 %all-gather = f32[128,4,8,8]{3,2,1,0:T(8,128)S(1)} all-gather(f32[16,4,8,8]{3,2,1,0:T(8,128)S(1)} %copy-done.2), channel_id=2, replica_groups=mesh['segment'=2,'group'=32,'tensor'=8] {'tensor'}, dimensions={0}, use_global_device_ids=true | all-gather | bytes 147456 | tf_op jit(solution)/shard_map/all_gather | solution.py:26
  409.9 215.9 %all-gather.8.cloned.1.call-done = f32[128,4,8,8,128]{4,3,2,1,0:T(8,128)} async-done(((f32[16,4,8,8,128]{4,3,2,1,0:T(8,128)}), f32[128,4,8,8,128]{4,3,2,1,0:T(8,128)}) %all-gather.8.cloned.1.call-update) | async-done | bytes 16777232 | tf_op jit(solution)/shard_map/all_gather | solution.py:26
  627.5 35.4 %while.19 = (s32[]{:T(128)}, f32[16,4,8,8]{0,3,2,1:T(8,128)}, f32[16,4,8,8]{0,3,2,1:T(8,128)}, f32[16,4,8,8,128]{4,3,2,1,0:T(8,128)S(1)}, f32[8,16,4,8,8]{1,4,3,...) while((s32[]{:T(128)}, f32[16,4,8,8]{0,3,2,1:T(8,128)}, ...), condition=%wide.region_19.20_spmd, body=%wide.region_18.19_spmd.sunk | while | flops 1597445 | bytes 6520983 | solution.py:32
  629.9 2.7 fusion.52
  634.9 2.7 fusion.52
  640.0 2.7 fusion.52
  645.1 2.7 fusion.52
  650.1 2.7 fusion.52
  655.2 2.7 fusion.52
  660.2 2.7 fusion.52
  (110 shorter events, 52.6 us)
Async XLA Ops:
  7.2 211.3 %copy-start = (bf16[384,1024]{1,0:T(8,128)(2,1)S(1)}, bf16[384,1024]{1,0:T(8,128)(2,1)}, u32[]{:S(2)}) copy-start(bf16[384,1024]{1,0:T(8,128)(2,1)} %param.15) | copy-start | bytes 2359300
  7.2 75.5 %copy-start.8 = (bf16[3,128,256]{2,1,0:T(8,128)(2,1)S(1)}, bf16[3,128,256]{2,1,0:T(8,128)(2,1)}, u32[]{:S(2)}) copy-start(bf16[3,128,256]{2,1,0:T(8,128)(2,1)} %param.18) | copy-start | bytes 589828
  7.2 75.9 %copy-start.4 = (bf16[384,256]{1,0:T(8,128)(2,1)S(1)}, bf16[384,256]{1,0:T(8,128)(2,1)}, u32[]{:S(2)}) copy-start(bf16[384,256]{1,0:T(8,128)(2,1)} %param.16) | copy-start | bytes 589828
  7.2 201.2 %all-gather.6.cloned.1.call-start = ((), (), s32[]{:S(2)}) async-start(), calls=%async_computation.2 | async-start | bytes 1179648 | tf_op jit(solution)/shard_map/all_gather | solution.py:179
  83.2 30.5 %copy-start.6 = (s32[64,16]{0,1:T(8,128)S(1)}, s32[64,16]{0,1:T(8,128)}, u32[]{:S(2)}) copy-start(s32[64,16]{0,1:T(8,128)} %param.22) | copy-start | bytes 12292
  88.2 65.3 %copy-start.1 = (bf16[16,32,2048]{2,1,0:T(8,128)(2,1)S(1)}, bf16[16,32,2048]{2,1,0:T(8,128)(2,1)}, u32[]{:S(2)}) copy-start(bf16[16,32,2048]{2,1,0:T(8,128)(2,1)} %param.23) | copy-start | bytes 6291460
  88.2 41.7 %collective-permute-start = (bf16[32,1,32,256]{3,2,1,0:T(8,128)(2,1)}, bf16[32,1,32,256]{3,2,1,0:T(8,128)(2,1)}, u32[]{:S(2)}, u32[]{:S(2)}) collective-permute-start(bf16[32,1,32,256]{3,2,1,0:T(8,128)(2,1)} %broadcast_select_fusion), channel_id=1, source_target_pairs={{0,256},{256,0},{1,257},{257,1},{2,258},{258,2},{3,259},{259,3},{4... | collective-permute-start | bytes 1572872 | tf_op jit(solution)/shard_map/ppermute | solution.py:22
  129.9 17.0 %all-to-all-start = ((bf16[32,1,32,256]{3,2,1,0:T(8,128)(2,1)}), bf16[32,1,32,256]{3,2,1,0:T(8,128)(2,1)}, u32[]{:S(2)}, u32[]{:S(2)}) async-start(bf16[32,1,32,256]{3,2,1,0:T(8,128)(2,1)} %collective-permute-done), calls=%async_computation | async-start | bytes 1048576 | tf_op jit(solution)/shard_map/all_to_all | solution.py:158
  149.4 61.5 %all-to-all-start.1 = ((bf16[16,32,256]{2,0,1:T(8,128)(2,1)}), bf16[16,32,256]{2,0,1:T(8,128)(2,1)}, u32[]{:S(2)}, u32[]{:S(2)}) async-start(bf16[16,32,256]{2,0,1:T(8,128)(2,1)} %copy.138), calls=%async_computation.1 | async-start | bytes 524288 | tf_op jit(solution)/shard_map/all_to_all | solution.py:174
  153.4 472.4 %all-gather.8.cloned.1.call-start = ((), (), s32[]{:S(2)}) async-start(), calls=%async_computation.3 | async-start | bytes 18874368 | tf_op jit(solution)/shard_map/all_gather | solution.py:26
  156.2 2.2 copy-start.5
  156.2 51.7 %copy-start.7 = (s32[64,16]{0,1:T(8,128)S(1)}, s32[64,16]{0,1:T(8,128)}, u32[]{:S(2)}) copy-start(s32[64,16]{0,1:T(8,128)} %param.21) | copy-start | bytes 12292
  212.1 1.2 copy-start.3
  316.4 2.8 copy-start.2
Sparse Core Ops, SparseCore 0:
  113.8 59.7 all-gather.5
  218.3 407.4 all-gather.7
where the time goes:
time: 678 us; the launch traced here: 675 us
  blocking collectives  294 us (43%)
  waiting for transfers between devices  241 us (36%)
  other arithmetic  40.9 us (6%)
  local copies, waits for them, and re-layouts  37.5 us (6%)
  starting transfers between devices  37.2 us (5%)
  between operations  14.4 us (2%)
  matrix products  9.07 us (1%)
    all_gather x1, waiting for transfers between devices, combined_all(): everything = jax.tree.map(lambda part: lax.all_gather(part, axis), shard)  216 us
    all_gather x2, blocking collectives, combined_all(): everything = jax.tree.map(lambda part: lax.all_gather(part, axis), shard)  177 us
    psum x1, blocking collectives, body(): summed = lax.psum(selected, 'tensor')  70 us
    all_gather x1, blocking collectives, body(): lax.all_gather(draft_key_values, 'tensor', axis=1, tiled=True)  47.5 us
    ppermute x1, starting transfers between devices, from_partner(): return lax.ppermute(block, axis, route)  25.5 us
    add x7, other arithmetic, combine_parts(): numer_one * factor_one[..., None] + numer_two * factor_two[..., None]  18.8 us
    ppermute x1, waiting for transfers between devices, from_partner(): return lax.ppermute(block, axis, route)  15.9 us
  transfers between devices with their start and end apart: 5, of which 3 were waited for; matrix products, arithmetic and copies ran while one was open for 4% of the time, Pallas kernels for 0%

commit v1 on v0

v1 whole, which is shorter than its diff:
```python
import jax
import jax.numpy as jnp
from jax import lax
from jax.experimental import pallas as pl
from jax.experimental.pallas import tpu as pltpu
from jax.sharding import PartitionSpec as P

HEAD = 128
GQA = 8
SPEC = 4
MAXLEN = 32
REQ = 16
NT = 8
NG = 32
TOK = 384
BLK = TOK // NT
ADAPTERS = 3
PARTS = 4
QROWS = REQ * SPEC // PARTS
KVW = 2 * HEAD
MSG = HEAD + 16
TILE = 96
SCALE = HEAD**-0.5
NEG = -1e30
MESH = pl.DeviceIdType.MESH
F32 = jnp.float32
BF16 = jnp.bfloat16


def nt_dot(a, b):
    return lax.dot_general(a, b, (((1,), (1,)), ((), ())), preferred_element_type=F32)


def tn_dot(a, b):
    return lax.dot_general(a, b, (((0,), (0,)), ((), ())), preferred_element_type=F32)


def iota(shape, dim):
    return lax.broadcasted_iota(jnp.int32, shape, dim)


def merge(a, b):
    num_a, m_a, l_a = a
    num_b, m_b, l_b = b
    m = jnp.maximum(m_a, m_b)
    f_a = jnp.exp(m_a - m)
    f_b = jnp.exp(m_b - m)
    return num_a * f_a + num_b * f_b, m, l_a * f_a + l_b * f_b


def partial_attention(keys, values, queries, mask):
    s = nt_dot(keys, queries) * SCALE
    s = jnp.where(mask, s, NEG)
    m = jnp.max(s, axis=0, keepdims=True).astype(BF16).astype(F32)
    p = jnp.where(mask, jnp.exp(s - m), 0.0)
    total = jnp.sum(p, axis=0, keepdims=True)
    num = tn_dot(values, p.astype(BF16))
    return num, m, total


def request_rows(lens, owner, row):
    lane = iota((1, 128), 1)
    start_row = jnp.full((1, 128), 1 << 20, jnp.int32)
    end_row = jnp.full((1, 128), 1 << 20, jnp.int32)
    owner_row = jnp.full((1, 128), -1, jnp.int32)
    at = jnp.int32(0)
    for i in range(REQ):
        n = lens[row, i]
        start_row = jnp.where(lane == i, at, start_row)
        at = at + n
        end_row = jnp.where(lane == i, at, end_row)
        owner_row = jnp.where(lane == i, owner[row, i], owner_row)
    return start_row, end_row, owner_row


def token_columns(start_row, end_row, tenant_row, ranks):
    pos = iota((TOK, 128), 0)
    hit = (pos >= start_row) & (pos < end_row)
    start = jnp.sum(jnp.where(hit, start_row.astype(F32), 0.0), axis=1, keepdims=True)
    adapter = jnp.sum(jnp.where(hit, tenant_row.astype(F32), 0.0), axis=1, keepdims=True)
    rank = jnp.zeros((TOK, 1), F32)
    for a in range(ADAPTERS):
        rank = jnp.where(adapter == float(a), ranks[a].astype(F32), rank)
    return start, adapter, rank


def kernel(
    hid, pq, pkv, down, up, ranks, tenant, lens, owner, cache, dq, dkv,
    pout, dout,
    hid_v, pq_v, pkv_v, down_v, up_v, cache_v, dkv_v, qall,
    own_num, own_st, sendb, recv_r, recv_l,
    rs_send, rs_recv, sh_own, sh_oth, pkv_o, ten_own, ten_oth,
    kv_own, packed, handed, acc, acc_st, pout_v, dout_v, slot_tab,
    lsem, qs, qr, ps, pr, rss, rsr, ags, agr, xs, xr, hs, hr, osem,
):
    s = lax.axis_index("segment")
    g = lax.axis_index("group")
    t = lax.axis_index("tensor")

    loads = []
    for k, (src, dst) in enumerate(
        [(dq, qall.at[t]), (hid, hid_v), (down, down_v), (pkv, pkv_v), (up, up_v),
         (cache, cache_v), (dkv, dkv_v), (pq, pq_v)]
    ):
        c = pltpu.make_async_copy(src, dst, lsem.at[k])
        c.start()
        loads.append(c)
    ld_q, ld_hid, ld_down, ld_pkv, ld_up, ld_cache, ld_dkv, ld_pq = loads

    barrier = pltpu.get_barrier_semaphore()

    def greet_tensor(k, _):
        pl.semaphore_signal(barrier, inc=1, device_id={"tensor": lax.rem(t + k, NT)}, device_id_type=MESH)
        return _

    def greet_cross(k, _):
        pl.semaphore_signal(
            barrier, inc=1, device_id={"segment": 1 - s, "tensor": lax.rem(t + k, NT)}, device_id_type=MESH
        )
        return _

    def greet_group(k, _):
        pl.semaphore_signal(barrier, inc=1, device_id={"group": lax.rem(g + k, NG)}, device_id_type=MESH)
        return _

    lax.fori_loop(1, NT, greet_tensor, 0)
    lax.fori_loop(0, NT, greet_cross, 0)
    lax.fori_loop(1, NG, greet_group, 0)

    here = s * NG + g
    there = (1 - s) * NG + g
    lane = iota((8, 128), 1)
    tenants = jnp.zeros((8, 128), jnp.int32)
    for i in range(REQ):
        tenants = jnp.where(lane == i, tenant[0, i], tenants)
    ten_own[...] = tenants
    start_row, end_row, _ = request_rows(lens, owner, here)
    start, adapter, rank = token_columns(start_row, end_row, tenants[0:1], ranks)

    pl.semaphore_wait(barrier, (NT - 1) + NT + (NG - 1))

    def q_copy(j, c, side):
        rows = pl.ds(c * QROWS, QROWS)
        return pltpu.make_async_remote_copy(
            src_ref=qall.at[j, rows],
            dst_ref=qall.at[j, rows],
            send_sem=qs.at[side, j, c],
            recv_sem=qr.at[j, c],
            device_id={"tensor": lax.rem(t + (1 if side == 0 else NT - 1), NT)},
            device_id_type=MESH,
        )

    def p_copy(j, c, side):
        return pltpu.make_async_remote_copy(
            src_ref=sendb.at[j, c],
            dst_ref=(recv_r if side == 0 else recv_l).at[j, c],
            send_sem=ps.at[side, j, c],
            recv_sem=pr.at[side, j, c],
            device_id={"tensor": lax.rem(t + (1 if side == 0 else NT - 1), NT)},
            device_id_type=MESH,
        )

    def rs_copy(k, src):
        return pltpu.make_async_remote_copy(
            src_ref=rs_send.at[k],
            dst_ref=rs_recv.at[src],
            send_sem=rss.at[k],
            recv_sem=rsr.at[src],
            device_id={"tensor": k},
            device_id_type=MESH,
        )

    def ag_copy(k, src):
        return pltpu.make_async_remote_copy(
            src_ref=sh_own.at[src],
            dst_ref=sh_own.at[src],
            send_sem=ags.at[0, k],
            recv_sem=agr.at[0, src],
            device_id={"tensor": k},
            device_id_type=MESH,
        )

    def cross_copy(k, src):
        return pltpu.make_async_remote_copy(
            src_ref=sh_own.at[src],
            dst_ref=sh_oth.at[src],
            send_sem=ags.at[1, k],
            recv_sem=agr.at[1, src],
            device_id={"segment": 1 - s, "tensor": k},
            device_id_type=MESH,
        )

    def base_copy():
        return pltpu.make_async_remote_copy(
            src_ref=pkv_v,
            dst_ref=pkv_o,
            send_sem=xs.at[0],
            recv_sem=xr.at[0],
            device_id={"segment": 1 - s},
            device_id_type=MESH,
        )

    def tenant_copy():
        return pltpu.make_async_remote_copy(
            src_ref=ten_own,
            dst_ref=ten_oth,
            send_sem=xs.at[1],
            recv_sem=xr.at[1],
            device_id={"segment": 1 - s},
            device_id_type=MESH,
        )

    def hand_copy(d, src):
        return pltpu.make_async_remote_copy(
            src_ref=packed.at[d],
            dst_ref=handed.at[src],
            send_sem=hs.at[d],
            recv_sem=hr.at[src],
            device_id={"group": d},
            device_id_type=MESH,
        )

    ld_q.wait()

    @pl.when(t < NT - 1)
    def _():
        for c in range(PARTS):
            q_copy(t, c, 0).start()

    @pl.when(t > 0)
    def _():
        for c in range(PARTS):
            q_copy(t, c, 1).start()

    ld_pkv.wait()
    tenant_copy().start()
    base_copy().start()

    ld_hid.wait()
    ld_down.wait()
    col = iota((TOK, HEAD), 1)
    selected = jnp.zeros((TOK, HEAD), F32)
    for a in range(ADAPTERS):
        part = jnp.dot(hid_v[...], down_v[a], preferred_element_type=F32)
        selected = jnp.where(adapter == float(a), part, selected)
    selected = jnp.where(col.astype(F32) < rank, selected, 0.0)
    rs_send[...] = selected.reshape(NT, BLK, HEAD)

    def rs_start(k, _):
        rs_copy(lax.rem(t + k, NT), t).start()
        return _

    lax.fori_loop(1, NT, rs_start, 0)

    def reduce_and_share():
        def add(k, total):
            src = lax.rem(t + k, NT)
            rs_copy(src, src).wait_recv()
            return total + rs_recv[src]

        total = lax.fori_loop(1, NT, add, rs_send[t])
        sh_own[t] = total.astype(BF16)

        def share(k, _):
            to = lax.rem(t + k, NT)
            ag_copy(to, t).start()
            cross_copy(to, t).start()
            return _

        lax.fori_loop(1, NT, share, 0)
        cross_copy(t, t).start()

    def lora_rows(shrunk, base, adapter_col, rank_col):
        delta = jnp.zeros((TOK, KVW), F32)
        for a in range(ADAPTERS):
            part = jnp.dot(shrunk, up_v[a], preferred_element_type=F32)
            delta = jnp.where(adapter_col == float(a), part, delta)
        return (base.astype(F32) + (8.0 / jnp.sqrt(rank_col)) * delta).astype(BF16)

    def hand_over():
        start_p, end_p, owner_p = request_rows(lens, owner, there)
        group_of = iota((NG * MAXLEN, 128), 0) // MAXLEN
        code = (start_p * 64 + (end_p - start_p)).astype(F32)
        found = jnp.sum(jnp.where(group_of == owner_p, code, 0.0), axis=1, keepdims=True)
        found = found.astype(jnp.int32)
        offset = iota((NG * MAXLEN, 1), 0) % MAXLEN
        source = jnp.where(offset < found % 64, found // 64 + offset, -1)
        pick = (iota((NG * MAXLEN, TOK), 1) == source).astype(F32).astype(BF16)
        tenant_copy().wait_recv()
        _, adapter_p, rank_p = token_columns(start_p, end_p, ten_oth[0:1, :], ranks)
        base_copy().wait_recv()
        ld_up.wait()

        def arrive(k, _):
            src = lax.rem(t + k, NT)
            cross_copy(src, src).wait_recv()
            return _

        lax.fori_loop(0, NT, arrive, 0)
        rows = lora_rows(sh_oth[...].reshape(TOK, HEAD), pkv_o[...], adapter_p, rank_p)
        moved = jnp.dot(pick, rows, preferred_element_type=F32).astype(BF16)
        packed[...] = moved.reshape(NG, MAXLEN, KVW)

        def send(k, _):
            d = lax.rem(g + k, NG)
            hand_copy(d, g).start()
            return _

        lax.fori_loop(1, NG, send, 0)
        handed[g] = packed[g]

    def own_rows():
        def arrive(k, _):
            src = lax.rem(t + k, NT)
            ag_copy(src, src).wait_recv()
            return _

        lax.fori_loop(1, NT, arrive, 0)
        kv_own[...] = lora_rows(sh_own[...].reshape(TOK, HEAD), pkv_v[...], adapter, rank)

    def prompt_tile(n):
        low = max(n * TILE - 32, 0)
        keys = kv_own[low:low + 128, 0:HEAD]
        values = kv_own[low:low + 128, HEAD:KVW]
        q_pos = iota((TILE, 128), 0) + n * TILE
        k_pos = iota((TILE, 128), 1) + low
        first = start[n * TILE:(n + 1) * TILE].astype(jnp.int32)
        mask = (k_pos >= first) & (k_pos <= q_pos)
        for h in range(GQA):
            q = pq_v[n * TILE:(n + 1) * TILE, h * HEAD:(h + 1) * HEAD]
            sc = jnp.where(mask, nt_dot(q, keys) * SCALE, NEG)
            e = jnp.exp(sc - jnp.max(sc, axis=1, keepdims=True))
            w = (e / jnp.sum(e, axis=1, keepdims=True)).astype(BF16)
            o = jnp.dot(w, values, preferred_element_type=F32)
            pout_v[n * TILE:(n + 1) * TILE, h * HEAD:(h + 1) * HEAD] = o.astype(BF16)

    def out_copy(n):
        rows = pl.ds(n * TILE, TILE)
        return pltpu.make_async_copy(pout_v.at[rows], pout.at[rows], osem.at[n])

    q_lane = iota((128, 128), 1) % QROWS
    k_row = iota((128, 128), 0)
    same_slot = (k_row // MAXLEN) == (q_lane // SPEC)

    def stacked(j, part):
        rows = slice(part * QROWS, (part + 1) * QROWS)
        return jnp.concatenate([qall[j, rows, h * HEAD:(h + 1) * HEAD] for h in range(GQA)], axis=0)

    def cached_partial(j, part):
        at = pl.multiple_of(j * KVW, KVW)
        slots = slice(part * 4, part * 4 + 4)
        keys = cache_v[slots, :, pl.ds(at, HEAD)].reshape(128, HEAD)
        values = cache_v[slots, :, pl.ds(at + HEAD, HEAD)].reshape(128, HEAD)
        return partial_attention(keys, values, stacked(j, part), same_slot)

    def put_message(j, part, num, m, total):
        high = total.astype(BF16)
        low = (total - high.astype(F32)).astype(BF16)
        sendb[j, part, 0:HEAD, :] = num.astype(BF16)
        row = iota((16, 128), 0)
        stats = jnp.where(row == 0, m, jnp.where(row == 1, high.astype(F32), low.astype(F32)))
        sendb[j, part, HEAD:MSG, :] = stats.astype(BF16)

    def get_message(buf, j, part):
        stats = buf[j, part, HEAD:MSG, :].astype(F32)
        return buf[j, part, 0:HEAD, :].astype(F32), stats[0:1], stats[1:2] + stats[2:3]

    def own_partial(j, part):
        return own_num[j, part], own_st[j, part, 0:1, :], own_st[j, part, 1:2, :]

    def attend_head(j):
        for part in range(PARTS):
            num, m, total = cached_partial(j, part)
            own_num[j, part] = num
            own_st[j, part, 0:1, :] = m
            own_st[j, part, 1:2, :] = total

    def first_link(j, side):
        for part in range(PARTS):
            put_message(j, part, *own_partial(j, part))
            p_copy(j, part, side).start()

    def next_link(j, side):
        buf = recv_r if side == 0 else recv_l
        for part in range(PARTS):
            p_copy(j, part, side).wait_recv()
            put_message(j, part, *merge(get_message(buf, j, part), own_partial(j, part)))
            p_copy(j, part, side).start()

    def put_acc(part, num, m, total):
        acc[part] = num
        acc_st[part, 0:1, :] = m
        acc_st[part, 1:2, :] = total

    def get_acc(part):
        return acc[part], acc_st[part, 0:1, :], acc_st[part, 1:2, :]

    def own_and_drafts():
        k_draft = iota((QROWS, 128), 0)
        q_draft = iota((QROWS, 128), 1) % QROWS
        mask = (k_draft // SPEC == q_draft // SPEC) & (k_draft % SPEC <= q_draft % SPEC)
        for part in range(PARTS):
            rows = slice(part * QROWS, (part + 1) * QROWS)
            draft = partial_attention(
                dkv_v[rows, 0:HEAD], dkv_v[rows, HEAD:KVW], stacked(t, part), mask
            )
            put_acc(part, *merge(cached_partial(t, part), draft))

    def find_slots():
        other = (1 - s) * NG
        for i in range(REQ):
            def look(k, src):
                return jnp.where(owner[other + k, i] == g, k, src)

            src = lax.fori_loop(0, NG, look, jnp.int32(0), unroll=True)
            slot_tab[0, i] = src
            slot_tab[1, i] = lens[other + src, i]

    def handed_attention():
        def arrive(k, _):
            src = lax.rem(g + k, NG)
            hand_copy(src, src).wait_recv()
            return _

        lax.fori_loop(1, NG, arrive, 0)
        for part in range(PARTS):
            keys, values = [], []
            limit = jnp.zeros((128, 128), jnp.int32)
            for u in range(4):
                i = part * 4 + u
                block = handed[slot_tab[0, i]]
                keys.append(block[:, 0:HEAD])
                values.append(block[:, HEAD:KVW])
                limit = jnp.where(k_row // MAXLEN == u, slot_tab[1, i], limit)
            mask = same_slot & (k_row % MAXLEN < limit)
            found = partial_attention(
                jnp.concatenate(keys, axis=0), jnp.concatenate(values, axis=0), stacked(t, part), mask
            )
            put_acc(part, *merge(get_acc(part), found))

    def finish(side):
        buf = recv_r if side == 0 else recv_l
        for part in range(PARTS):
            p_copy(t, part, side).wait_recv()
            put_acc(part, *merge(get_acc(part), get_message(buf, t, part)))

    def step(tau, carry):
        from_right = t + tau
        from_left = t - tau

        @pl.when(from_right < NT)
        def _():
            for c in range(PARTS):
                q_copy(from_right, c, 1).wait_recv()

                @pl.when(t > 0)
                def _():
                    q_copy(from_right, c, 1).start()

        @pl.when(from_left >= 0)
        def _():
            for c in range(PARTS):
                q_copy(from_left, c, 0).wait_recv()

                @pl.when(t < NT - 1)
                def _():
                    q_copy(from_left, c, 0).start()

        @pl.when(tau == 1)
        def _():
            reduce_and_share()
            ld_cache.wait()

        @pl.when(from_right < NT)
        def _():
            attend_head(from_right)

            @pl.when(t == 0)
            def _():
                first_link(from_right, 0)

        @pl.when(from_left >= 0)
        def _():
            attend_head(from_left)

            @pl.when(t == NT - 1)
            def _():
                first_link(from_left, 1)

        to_right = tau - t

        @pl.when((t >= 1) & (to_right > t) & (to_right < NT))
        def _():
            next_link(to_right, 0)

        to_left = 2 * (NT - 1) - t - tau

        @pl.when((t <= NT - 2) & (to_left < t) & (to_left >= 0))
        def _():
            next_link(to_left, 1)

        @pl.when(tau == 2)
        def _():
            hand_over()

        @pl.when(tau == 3)
        def _():
            own_rows()
            ld_pq.wait()
            ld_dkv.wait()

        for n in range(TOK // TILE):
            @pl.when(tau == 4 + n)
            def _():
                prompt_tile(n)
                out_copy(n).start()

        @pl.when(tau == 8)
        def _():
            own_and_drafts()
            find_slots()

        @pl.when(tau == 9)
        def _():
            handed_attention()

        return carry

    lax.fori_loop(1, 2 * NT - 1, step, 0)

    @pl.when(t > 0)
    def _():
        finish(0)

    @pl.when(t < NT - 1)
    def _():
        finish(1)

    for part in range(PARTS):
        num, _, total = get_acc(part)
        out = jnp.transpose(num / total)
        for h in range(GQA):
            dout_v[part * QROWS:(part + 1) * QROWS, h * HEAD:(h + 1) * HEAD] = out[
                h * QROWS:(h + 1) * QROWS
            ].astype(BF16)
    last = pltpu.make_async_copy(dout_v, dout, osem.at[TOK // TILE])
    last.start()

    for side in range(2):
        edge = (t < NT - 1) if side == 0 else (t > 0)

        @pl.when(edge)
        def _(side=side):
            def each(j, carry):
                @pl.when((j <= t) if side == 0 else (j >= t))
                def _():
                    for c in range(PARTS):
                        q_copy(j, c, side).wait_send()

                @pl.when((j > t) if side == 0 else (j < t))
                def _():
                    for c in range(PARTS):
                        p_copy(j, c, side).wait_send()

                return carry

            lax.fori_loop(0, NT, each, 0)

    def left_tensor(k, _):
        to = lax.rem(t + k, NT)
        rs_copy(to, t).wait_send()
        ag_copy(to, t).wait_send()
        cross_copy(to, t).wait_send()
        return _

    lax.fori_loop(1, NT, left_tensor, 0)
    cross_copy(t, t).wait_send()
    base_copy().wait_send()
    tenant_copy().wait_send()

    def left_group(k, _):
        hand_copy(lax.rem(g + k, NG), g).wait_send()
        return _

    lax.fori_loop(1, NG, left_group, 0)
    for n in range(TOK // TILE):
        out_copy(n).wait()
    last.wait()


def body(*args):
    any_space = pl.BlockSpec(memory_space=pl.ANY)
    smem = pl.BlockSpec(memory_space=pltpu.SMEM)
    dma = pltpu.SemaphoreType.DMA
    return pl.pallas_call(
        kernel,
        out_shape=(
            jax.ShapeDtypeStruct((TOK, GQA * HEAD), BF16),
            jax.ShapeDtypeStruct((REQ * SPEC, GQA * HEAD), BF16),
        ),
        in_specs=[any_space] * 5 + [smem] * 4 + [any_space] * 3,
        out_specs=(any_space, any_space),
        scratch_shapes=[
            pltpu.VMEM((TOK, NT * HEAD), BF16),
            pltpu.VMEM((TOK, GQA * HEAD), BF16),
            pltpu.VMEM((TOK, KVW), BF16),
            pltpu.VMEM((ADAPTERS, NT * HEAD, HEAD), BF16),
            pltpu.VMEM((ADAPTERS, HEAD, KVW), BF16),
            pltpu.VMEM((REQ, 32, NT * KVW), BF16),
            pltpu.VMEM((REQ * SPEC, KVW), BF16),
            pltpu.VMEM((NT, REQ * SPEC, GQA * HEAD), BF16),
            pltpu.VMEM((NT, PARTS, HEAD, 128), F32),
            pltpu.VMEM((NT, PARTS, 8, 128), F32),
            pltpu.VMEM((NT, PARTS, MSG, 128), BF16),
            pltpu.VMEM((NT, PARTS, MSG, 128), BF16),
            pltpu.VMEM((NT, PARTS, MSG, 128), BF16),
            pltpu.VMEM((NT, BLK, HEAD), F32),
            pltpu.VMEM((NT, BLK, HEAD), F32),
            pltpu.VMEM((NT, BLK, HEAD), BF16),
            pltpu.VMEM((NT, BLK, HEAD), BF16),
            pltpu.VMEM((TOK, KVW), BF16),
            pltpu.VMEM((8, 128), jnp.int32),
            pltpu.VMEM((8, 128), jnp.int32),
            pltpu.VMEM((TOK, KVW), BF16),
            pltpu.VMEM((NG, MAXLEN, KVW), BF16),
            pltpu.VMEM((NG, MAXLEN, KVW), BF16),
            pltpu.VMEM((PARTS, HEAD, 128), F32),
            pltpu.VMEM((PARTS, 8, 128), F32),
            pltpu.VMEM((TOK, GQA * HEAD), BF16),
            pltpu.VMEM((REQ * SPEC, GQA * HEAD), BF16),
            pltpu.SMEM((2, REQ), jnp.int32),
            dma((8,)),
            dma((2, NT, PARTS)),
            dma((NT, PARTS)),
            dma((2, NT, PARTS)),
            dma((2, NT, PARTS)),
            dma((NT,)),
            dma((NT,)),
            dma((2, NT)),
            dma((2, NT)),
            dma((2,)),
            dma((2,)),
            dma((NG,)),
            dma((NG,)),
            dma((TOK // TILE + 1,)),
        ],
        compiler_params=pltpu.CompilerParams(
            collective_id=0, has_side_effects=True, vmem_limit_bytes=40 << 20
        ),
    )(*args)


def solution(mesh):
    rows = ("segment", "group")
    return jax.shard_map(
        body,
        mesh=mesh,
        in_specs=(
            P(rows, "tensor"),
            P(rows, "tensor"),
            P(rows, "tensor"),
            P(None, "tensor", None),
            P(None, None, "tensor"),
            P(),
            P(rows, None),
            P(),
            P(),
            P(rows, "tensor", None),
            P(rows, "tensor"),
            P(rows, "tensor"),
        ),
        out_specs=(P(rows, "tensor"), P(rows, "tensor")),
        check_vma=False,
    )
```

time: 678 us -> 126 us (0.19)
  blocking collectives: 294 us -> 0 us
  waiting for transfers between devices: 241 us -> 0 us
  Pallas kernels: 0 us -> 112 us
  other arithmetic: 40.9 us -> 0 us
  starting transfers between devices: 37.2 us -> 0 us
  local copies, waits for them, and re-layouts: 37.5 us -> 12.9 us
  between operations: 14.4 us -> 0.65 us
  matrix products: 9.07 us -> 0 us
    all_gather x3 -> x0, blocking collectives: 224 us -> none  [the longest x2 177 us: combined_all(): everything = jax.tree.map(lambda part: lax.all_gather(part, axis), shard)]
    all_gather x2 -> x0, waiting for transfers between devices: 216 us -> none  [the longest x1 216 us: combined_all(): everything = jax.tree.map(lambda part: lax.all_gather(part, axis), shard)]
    pallas_call x0 -> x1, Pallas kernels: none -> 112 us  [body(): pl.pallas_call(kernel, out_shape=(jax.ShapeDtypeStruct((TOK, GQA * HEAD),...]
    psum x1 -> x0, blocking collectives: 70 us -> none  [body(): summed = lax.psum(selected, 'tensor')]
    add x15 -> x0, other arithmetic: 31.6 us -> none  [the longest x7 18.8 us: combine_parts(): numer_one * factor_one[..., None] + numer_two * factor_two[..., None]]
    ppermute x1 -> x0, starting transfers between devices: 25.5 us -> none  [from_partner(): return lax.ppermute(block, axis, route)]
    ppermute x1 -> x0, waiting for transfers between devices: 15.9 us -> none  [from_partner(): return lax.ppermute(block, axis, route)]
    all_to_all x2 -> x0, starting transfers between devices: 11.7 us -> none  [the longest x1 7.63 us: body(): lax.all_to_all(crossed, 'group', split_axis=0, concat_axis=0, tiled=True)]
  transfers between devices with their start and end apart: 5 -> 0, of which waited for: 3 -> 0; matrix products, arithmetic and copies ran while one was open for 4% -> 0% of each run, Pallas kernels for 0% -> 0%
where the time goes in v1:
time: 126 us; the launch traced here: 125 us
  Pallas kernels  112 us (89%)
  local copies, waits for them, and re-layouts  12.9 us (10%)
    pallas_call x1, Pallas kernels, body(): pl.pallas_call(kernel, out_shape=(jax.ShapeDtypeStruct((TOK, GQA * HEAD),...  112 us
    unnamed x24, local copies, waits for them, and re-layouts  12.9 us

profile of v1, /device:TPU:6, one launch (start us, length us, event | category | flops | bytes accessed | tf_op | source)
XLA Modules:
  0.0 125.1 jit_solution(16473211023384291036)
XLA Ops:
  0.6 0.8 copy.14.lens
  1.4 0.8 copy.15.owner
  2.2 0.0 copy-start
  2.2 1.6 %copy-done = bf16[16,32,2048]{2,1,0:T(8,128)(2,1)S(1)} copy-done((bf16[16,32,2048]{2,1,0:T(8,128)(2,1)S(1)}, bf16[16,32,2048]{2,1,0:T(8,128)(2,1)}, u32[]{:S(2)}) %copy-start) | copy-done | bytes 2097176
  3.8 0.0 copy-start.1
  3.8 1.1 copy-done.1
  4.9 0.0 copy-start.2
  4.9 1.1 copy-done.2
  6.0 0.0 copy-start.3
  6.1 1.1 copy-done.3
  7.2 0.0 copy-start.4
  7.2 0.9 copy-done.4
  8.1 0.0 copy-start.5
  8.1 0.9 copy-done.5
  9.0 0.0 copy-start.6
  9.0 0.9 copy-done.6
  9.9 0.0 copy-start.7
  9.9 0.8 copy-done.7
  10.7 0.0 copy-start.8
  10.7 0.7 copy-done.8
  11.4 0.7 copy-done.9
  12.0 111.6 %shard_map.131 = (bf16[384,1024]{1,0:T(8,128)(2,1)S(1)}, bf16[64,1024]{1,0:T(8,128)(2,1)S(1)}) custom-call(bf16[384,1024]{1,0:T(8,128)(2,1)S(1)} %copy-done.1, bf16[384,1024]{1,0:T(8,128)(2,1)S(1)} %copy-done.2, bf16[384,256]{1,0:T(8,128)(2,1)S(1)} %copy-done.4, bf16[3,1024,128]{2,1,0:T(8,128)(2,1)S(1)} %copy-done.3, bf16[3,128,256]{2,1,0:T(8,128)(2,1)S(1)} %copy-done.5, ...), custom_call_target="tpu_custom_call" | custom-call | tf_op jit(solution)/shard_map/pallas_call | solution.py:595
  123.6 0.9 copy.18
  124.5 0.7 copy.19
  (1 shorter events, 0.0 us)
Async XLA Ops:
  2.2 1.6 %copy-start = (bf16[16,32,2048]{2,1,0:T(8,128)(2,1)S(1)}, bf16[16,32,2048]{2,1,0:T(8,128)(2,1)}, u32[]{:S(2)}) copy-start(bf16[16,32,2048]{2,1,0:T(8,128)(2,1)} %cache.1) | copy-start | bytes 6291460
  3.8 1.1 copy-start.1
  4.9 1.1 copy-start.2
  6.0 1.1 copy-start.3
  7.2 0.9 copy-start.4
  8.1 0.9 copy-start.5
  9.0 0.9 copy-start.6
  9.9 0.8 copy-start.7
  10.7 0.7 copy-start.8
  11.4 0.7 copy-start.9

commit v2 on v1

v2 whole, which is shorter than its diff:
```python
import jax
import jax.numpy as jnp
from jax import lax
from jax.experimental import pallas as pl
from jax.experimental.pallas import tpu as pltpu
from jax.sharding import PartitionSpec as P

HEAD = 128
GQA = 8
SPEC = 4
MAXLEN = 32
REQ = 16
NT = 8
NG = 32
TOK = 384
BLK = TOK // NT
ADAPTERS = 3
PARTS = 4
QROWS = REQ * SPEC // PARTS
KVW = 2 * HEAD
STATS = 16
MSG = STATS + PARTS * HEAD
TILE = 96
SCALE = HEAD**-0.5
SHARE_AT = 3
OWN_AT = 5
HAND_AT = (9, 10)
TILE_AT = (6, 7, 8, 9)
HANDED_AT = 12
NEG = -1e30
MESH = pl.DeviceIdType.MESH
F32 = jnp.float32
BF16 = jnp.bfloat16


def nt_dot(a, b):
    return lax.dot_general(a, b, (((1,), (1,)), ((), ())), preferred_element_type=F32)


def tn_dot(a, b):
    return lax.dot_general(a, b, (((0,), (0,)), ((), ())), preferred_element_type=F32)


def iota(shape, dim):
    return lax.broadcasted_iota(jnp.int32, shape, dim)


def merge(a, b):
    num_a, m_a, l_a = a
    num_b, m_b, l_b = b
    m = jnp.maximum(m_a, m_b)
    f_a = jnp.exp(m_a - m)
    f_b = jnp.exp(m_b - m)
    return num_a * f_a + num_b * f_b, m, l_a * f_a + l_b * f_b


def partial_attention(keys, values, queries, mask):
    s = nt_dot(keys, queries) * SCALE
    s = jnp.where(mask, s, NEG)
    m = jnp.max(s, axis=0, keepdims=True).astype(BF16).astype(F32)
    p = jnp.where(mask, jnp.exp(s - m), 0.0)
    total = jnp.sum(p, axis=0, keepdims=True)
    num = tn_dot(values, p.astype(BF16))
    return num, m, total


def request_rows(lens, owner, row):
    lane = iota((1, 128), 1)
    start_row = jnp.full((1, 128), 1 << 20, jnp.int32)
    end_row = jnp.full((1, 128), 1 << 20, jnp.int32)
    owner_row = jnp.full((1, 128), -1, jnp.int32)
    at = jnp.int32(0)
    for i in range(REQ):
        n = lens[i, row]
        start_row = jnp.where(lane == i, at, start_row)
        at = at + n
        end_row = jnp.where(lane == i, at, end_row)
        owner_row = jnp.where(lane == i, owner[i, row], owner_row)
    return start_row, end_row, owner_row


def token_columns(start_row, end_row, tenant_row, ranks):
    pos = iota((TOK, 128), 0)
    hit = (pos >= start_row) & (pos < end_row)
    start = jnp.sum(jnp.where(hit, start_row.astype(F32), 0.0), axis=1, keepdims=True)
    adapter = jnp.sum(jnp.where(hit, tenant_row.astype(F32), 0.0), axis=1, keepdims=True)
    rank = jnp.zeros((TOK, 1), F32)
    for a in range(ADAPTERS):
        rank = jnp.where(adapter == float(a), ranks[a].astype(F32), rank)
    return start, adapter, rank


def kernel(
    hid, pq, pkv, down, up, ranks_h, tenant_h, lens_h, owner_h, cache, dq, dkv,
    pout, dout,
    hid_v, pq_v, pkv_v, down_v, up_v, cache_v, dkv_v, qall,
    own_num, own_st, sendb, recv_r, recv_l,
    mine, pick_v, rs_send, rs_recv, sh_own,
    kv_own, kv_oth, packed, handed, acc, acc_st, pout_v, dout_v, slot_tab,
    ranks, tenant, lens, owner,
    lsem, qs, qr, ps, pr, rss, rsr, ags, agr, xs, xr, hs, hr, osem,
):
    s = lax.axis_index("segment")
    g = lax.axis_index("group")
    t = lax.axis_index("tensor")

    loads = []
    for k, (src, dst) in enumerate(
        [(lens_h, lens), (owner_h, owner), (tenant_h, tenant), (ranks_h, ranks),
         (dq, qall.at[t]), (hid, hid_v), (down, down_v), (pkv, pkv_v), (up, up_v),
         (cache, cache_v), (dkv, dkv_v), (pq, pq_v)]
    ):
        c = pltpu.make_async_copy(src, dst, lsem.at[k])
        c.start()
        loads.append(c)
    ld_q, ld_hid, ld_down, ld_pkv, ld_up, ld_cache, ld_dkv, ld_pq = loads[4:]

    barrier = pltpu.get_barrier_semaphore()

    def greet_tensor(k, _):
        pl.semaphore_signal(barrier, inc=1, device_id={"tensor": lax.rem(t + k, NT)}, device_id_type=MESH)
        return _

    def greet_group(k, _):
        pl.semaphore_signal(barrier, inc=1, device_id={"group": lax.rem(g + k, NG)}, device_id_type=MESH)
        return _

    lax.fori_loop(1, NT, greet_tensor, 0)
    pl.semaphore_signal(barrier, inc=1, device_id={"segment": 1 - s}, device_id_type=MESH)
    lax.fori_loop(1, NG, greet_group, 0)

    for c in loads[:4]:
        c.wait()

    here = s * NG + g
    there = (1 - s) * NG + g
    lane = iota((8, 128), 1)
    tenants = jnp.zeros((8, 128), jnp.int32)
    for i in range(REQ):
        tenants = jnp.where(lane == i, tenant[0, i], tenants)
    start_row, end_row, _ = request_rows(lens, owner, here)
    start, adapter, rank = token_columns(start_row, end_row, tenants[0:1], ranks)

    ld_hid.wait()
    ld_down.wait()
    col = iota((TOK, HEAD), 1)
    selected = jnp.zeros((TOK, HEAD), F32)
    for a in range(ADAPTERS):
        part = jnp.dot(hid_v[...], down_v[a], preferred_element_type=F32)
        selected = jnp.where(adapter == float(a), part, selected)
    selected = jnp.where(col.astype(F32) < rank, selected, 0.0)
    mine[...] = selected.reshape(NT, BLK, HEAD)
    rs_send[...] = mine[...].astype(BF16)

    pl.semaphore_wait(barrier, (NT - 1) + 1 + (NG - 1))

    def q_copy(j, c, side):
        rows = pl.ds(c * QROWS, QROWS)
        return pltpu.make_async_remote_copy(
            src_ref=qall.at[j, rows],
            dst_ref=qall.at[j, rows],
            send_sem=qs.at[side, j, c],
            recv_sem=qr.at[j, c],
            device_id={"tensor": lax.rem(t + (1 if side == 0 else NT - 1), NT)},
            device_id_type=MESH,
        )

    def p_copy(j, c, side):
        rows = pl.ds(0, STATS + HEAD) if c == 0 else pl.ds(STATS + c * HEAD, HEAD)
        return pltpu.make_async_remote_copy(
            src_ref=sendb.at[j, rows],
            dst_ref=(recv_r if side == 0 else recv_l).at[j, rows],
            send_sem=ps.at[side, j, c],
            recv_sem=pr.at[side, j, c],
            device_id={"tensor": lax.rem(t + (1 if side == 0 else NT - 1), NT)},
            device_id_type=MESH,
        )

    def rs_copy(k, src):
        return pltpu.make_async_remote_copy(
            src_ref=rs_send.at[k],
            dst_ref=rs_recv.at[src],
            send_sem=rss.at[k],
            recv_sem=rsr.at[src],
            device_id={"tensor": k},
            device_id_type=MESH,
        )

    def ag_copy(k, src):
        return pltpu.make_async_remote_copy(
            src_ref=sh_own.at[src],
            dst_ref=sh_own.at[src],
            send_sem=ags.at[k],
            recv_sem=agr.at[src],
            device_id={"tensor": k},
            device_id_type=MESH,
        )

    def rows_copy(half):
        return pltpu.make_async_remote_copy(
            src_ref=kv_own.at[half],
            dst_ref=kv_oth.at[half],
            send_sem=xs.at[half],
            recv_sem=xr.at[half],
            device_id={"segment": 1 - s},
            device_id_type=MESH,
        )

    def hand_copy(half, d, src):
        return pltpu.make_async_remote_copy(
            src_ref=packed.at[half, d],
            dst_ref=handed.at[half, src],
            send_sem=hs.at[half, d],
            recv_sem=hr.at[half, src],
            device_id={"group": d},
            device_id_type=MESH,
        )

    def rs_start(k, _):
        rs_copy(lax.rem(t + k, NT), t).start()
        return _

    lax.fori_loop(1, NT, rs_start, 0)
    ld_q.wait()

    @pl.when(t < NT - 1)
    def _():
        for c in range(PARTS):
            q_copy(t, c, 0).start()

    @pl.when(t > 0)
    def _():
        for c in range(PARTS):
            q_copy(t, c, 1).start()

    def reduce_and_share():
        def add(k, total):
            src = lax.rem(t + k, NT)
            rs_copy(src, src).wait_recv()
            return total + rs_recv[src].astype(F32)

        total = lax.fori_loop(1, NT, add, mine[t])
        sh_own[t] = total.astype(BF16)

        def share(k, _):
            to = lax.rem(t + k, NT)
            ag_copy(to, t).start()
            return _

        lax.fori_loop(1, NT, share, 0)

    def lora_rows(shrunk, base, adapter_col, rank_col):
        delta = jnp.zeros((TOK, KVW), F32)
        for a in range(ADAPTERS):
            part = jnp.dot(shrunk, up_v[a], preferred_element_type=F32)
            delta = jnp.where(adapter_col == float(a), part, delta)
        return (base.astype(F32) + (8.0 / jnp.sqrt(rank_col)) * delta).astype(BF16)

    def find_rows():
        start_p, end_p, owner_p = request_rows(lens, owner, there)
        group_of = iota((NG * MAXLEN, 128), 0) // MAXLEN
        code = (start_p * 64 + (end_p - start_p)).astype(F32)
        found = jnp.sum(jnp.where(group_of == owner_p, code, 0.0), axis=1, keepdims=True)
        found = found.astype(jnp.int32)
        offset = iota((NG * MAXLEN, 1), 0) % MAXLEN
        source = jnp.where(offset < found % 64, found // 64 + offset, -1)
        pick_v[...] = (iota((NG * MAXLEN, TOK), 1) == source).astype(F32).astype(BF16)

    def hand_over(half):
        rows_copy(half).wait_recv()
        moved = jnp.dot(pick_v[...], kv_oth[half], preferred_element_type=F32).astype(BF16)
        packed[half] = moved.reshape(NG, MAXLEN, HEAD)

        def send(k, _):
            hand_copy(half, lax.rem(g + k, NG), g).start()
            return _

        lax.fori_loop(1, NG, send, 0)
        handed[half, g] = packed[half, g]

    def own_rows():
        def arrive(k, _):
            src = lax.rem(t + k, NT)
            ag_copy(src, src).wait_recv()
            return _

        lax.fori_loop(1, NT, arrive, 0)
        rows = lora_rows(sh_own[...].reshape(TOK, HEAD), pkv_v[...], adapter, rank)
        for half in range(2):
            kv_own[half] = rows[:, half * HEAD:(half + 1) * HEAD]
            rows_copy(half).start()

    def prompt_tile(n):
        low = max(n * TILE - 32, 0)
        keys = kv_own[0, low:low + 128]
        values = kv_own[1, low:low + 128]
        q_pos = iota((TILE, 128), 0) + n * TILE
        k_pos = iota((TILE, 128), 1) + low
        first = start[n * TILE:(n + 1) * TILE].astype(jnp.int32)
        mask = (k_pos >= first) & (k_pos <= q_pos)
        rows = slice(n * TILE, (n + 1) * TILE)
        q = jnp.concatenate([pq_v[rows, h * HEAD:(h + 1) * HEAD] for h in range(GQA)], axis=0)
        sc = (nt_dot(q, keys) * SCALE).reshape(GQA, TILE, 128)
        sc = jnp.where(mask[None], sc, NEG).reshape(GQA * TILE, 128)
        e = jnp.exp(sc - jnp.max(sc, axis=1, keepdims=True))
        w = (e * (1.0 / jnp.sum(e, axis=1, keepdims=True))).astype(BF16)
        o = jnp.dot(w, values, preferred_element_type=F32).astype(BF16)
        for h in range(GQA):
            pout_v[rows, h * HEAD:(h + 1) * HEAD] = o[h * TILE:(h + 1) * TILE]

    def out_copy(n):
        rows = pl.ds(n * TILE, TILE)
        return pltpu.make_async_copy(pout_v.at[rows], pout.at[rows], osem.at[n])

    q_lane = iota((128, 128), 1) % QROWS
    k_row = iota((128, 128), 0)
    same_slot = (k_row // MAXLEN) == (q_lane // SPEC)

    def stacked(j, part):
        rows = slice(part * QROWS, (part + 1) * QROWS)
        return jnp.concatenate([qall[j, rows, h * HEAD:(h + 1) * HEAD] for h in range(GQA)], axis=0)

    def cached_partial(j, part):
        at = pl.multiple_of(j * KVW, KVW)
        slots = slice(part * 4, part * 4 + 4)
        keys = cache_v[slots, :, pl.ds(at, HEAD)].reshape(128, HEAD)
        values = cache_v[slots, :, pl.ds(at + HEAD, HEAD)].reshape(128, HEAD)
        return partial_attention(keys, values, stacked(j, part), same_slot)

    def put_stats(j, stats):
        rows = []
        for m, total in stats:
            high = total.astype(BF16).astype(F32)
            rows += [m, high, total - high]
        rows.append(jnp.zeros((STATS - len(rows), 128), F32))
        sendb[j, 0:STATS, :] = jnp.concatenate(rows, axis=0).astype(BF16)

    def put_num(j, part, num):
        at = STATS + part * HEAD
        sendb[j, at:at + HEAD, :] = num.astype(BF16)

    def get_stats(buf, j):
        st = buf[j, 0:STATS, :].astype(F32)
        return [(st[3 * p:3 * p + 1], st[3 * p + 1:3 * p + 2] + st[3 * p + 2:3 * p + 3]) for p in range(PARTS)]

    def get_num(buf, j, part):
        at = STATS + part * HEAD
        return buf[j, at:at + HEAD, :].astype(F32)

    def own_partial(j, part):
        return own_num[j, part], own_st[j, part, 0:1, :], own_st[j, part, 1:2, :]

    def attend_head(j):
        for part in range(PARTS):
            num, m, total = cached_partial(j, part)
            own_num[j, part] = num
            own_st[j, part, 0:1, :] = m
            own_st[j, part, 1:2, :] = total

    def first_link(j, side):
        put_stats(j, [own_partial(j, part)[1:] for part in range(PARTS)])
        for part in range(PARTS):
            put_num(j, part, own_num[j, part])
            p_copy(j, part, side).start()

    def next_link(j, side):
        buf = recv_r if side == 0 else recv_l
        p_copy(j, 0, side).wait_recv()
        stats, factors = [], []
        for part, (m_in, total_in) in enumerate(get_stats(buf, j)):
            _, m_own, total_own = own_partial(j, part)
            m = jnp.maximum(m_in, m_own)
            f_in, f_own = jnp.exp(m_in - m), jnp.exp(m_own - m)
            stats.append((m, total_in * f_in + total_own * f_own))
            factors.append((f_in, f_own))
        put_stats(j, stats)
        for part, (f_in, f_own) in enumerate(factors):
            if part > 0:
                p_copy(j, part, side).wait_recv()
            put_num(j, part, get_num(buf, j, part) * f_in + own_num[j, part] * f_own)
            p_copy(j, part, side).start()

    def put_acc(part, num, m, total):
        acc[part] = num
        acc_st[part, 0:1, :] = m
        acc_st[part, 1:2, :] = total

    def get_acc(part):
        return acc[part], acc_st[part, 0:1, :], acc_st[part, 1:2, :]

    def own_and_drafts():
        k_draft = iota((QROWS, 128), 0)
        q_draft = iota((QROWS, 128), 1) % QROWS
        mask = (k_draft // SPEC == q_draft // SPEC) & (k_draft % SPEC <= q_draft % SPEC)
        for part in range(PARTS):
            rows = slice(part * QROWS, (part + 1) * QROWS)
            draft = partial_attention(
                dkv_v[rows, 0:HEAD], dkv_v[rows, HEAD:KVW], stacked(t, part), mask
            )
            put_acc(part, *merge(cached_partial(t, part), draft))

    def find_slots():
        other = (1 - s) * NG
        for i in range(REQ):
            def look(k, src):
                return jnp.where(owner[i, other + k] == g, k, src)

            src = lax.fori_loop(0, NG, look, jnp.int32(0), unroll=True)
            slot_tab[0, i] = src
            slot_tab[1, i] = lens[i, other + src]

    def handed_attention():
        def arrive(k, _):
            src = lax.rem(g + k, NG)
            hand_copy(0, src, src).wait_recv()
            hand_copy(1, src, src).wait_recv()
            return _

        lax.fori_loop(1, NG, arrive, 0)
        for part in range(PARTS):
            keys, values = [], []
            limit = jnp.zeros((128, 128), jnp.int32)
            for u in range(4):
                i = part * 4 + u
                keys.append(handed[0, slot_tab[0, i]])
                values.append(handed[1, slot_tab[0, i]])
                limit = jnp.where(k_row // MAXLEN == u, slot_tab[1, i], limit)
            mask = same_slot & (k_row % MAXLEN < limit)
            found = partial_attention(
                jnp.concatenate(keys, axis=0), jnp.concatenate(values, axis=0), stacked(t, part), mask
            )
            put_acc(part, *merge(get_acc(part), found))

    def finish(side):
        buf = recv_r if side == 0 else recv_l
        for part in range(PARTS):
            p_copy(t, part, side).wait_recv()
        stats = get_stats(buf, t)
        for part in range(PARTS):
            put_acc(part, *merge(get_acc(part), (get_num(buf, t, part), *stats[part])))

    def step(tau, carry):
        from_right = t + tau
        from_left = t - tau

        @pl.when(from_right < NT)
        def _():
            for c in range(PARTS):
                q_copy(from_right, c, 1).wait_recv()

                @pl.when(t > 0)
                def _():
                    q_copy(from_right, c, 1).start()

        @pl.when(from_left >= 0)
        def _():
            for c in range(PARTS):
                q_copy(from_left, c, 0).wait_recv()

                @pl.when(t < NT - 1)
                def _():
                    q_copy(from_left, c, 0).start()

        @pl.when(from_right < NT)
        def _():
            attend_head(from_right)

            @pl.when(t == 0)
            def _():
                first_link(from_right, 0)

        @pl.when(from_left >= 0)
        def _():
            attend_head(from_left)

            @pl.when(t == NT - 1)
            def _():
                first_link(from_left, 1)

        to_right = tau - t

        @pl.when((t >= 1) & (to_right > t) & (to_right < NT))
        def _():
            next_link(to_right, 0)

        to_left = 2 * (NT - 1) - t - tau

        @pl.when((t <= NT - 2) & (to_left < t) & (to_left >= 0))
        def _():
            next_link(to_left, 1)

        @pl.when(tau == SHARE_AT)
        def _():
            reduce_and_share()

        @pl.when(tau == OWN_AT)
        def _():
            own_rows()

        for half in range(2):
            @pl.when(tau == HAND_AT[half])
            def _(half=half):
                hand_over(half)

        for n in range(TOK // TILE):
            @pl.when(tau == TILE_AT[n])
            def _(n=n):
                prompt_tile(n)
                out_copy(n).start()

        @pl.when(tau == HANDED_AT)
        def _():
            handed_attention()

        return carry

    ld_cache.wait()
    ld_dkv.wait()
    ld_pkv.wait()
    ld_up.wait()
    ld_pq.wait()
    own_and_drafts()
    find_rows()
    find_slots()
    lax.fori_loop(1, 2 * NT - 1, step, 0)

    @pl.when(t > 0)
    def _():
        finish(0)

    @pl.when(t < NT - 1)
    def _():
        finish(1)

    for part in range(PARTS):
        num, _, total = get_acc(part)
        out = jnp.transpose(num / total)
        for h in range(GQA):
            dout_v[part * QROWS:(part + 1) * QROWS, h * HEAD:(h + 1) * HEAD] = out[
                h * QROWS:(h + 1) * QROWS
            ].astype(BF16)
    last = pltpu.make_async_copy(dout_v, dout, osem.at[TOK // TILE])
    last.start()

    for side in range(2):
        edge = (t < NT - 1) if side == 0 else (t > 0)

        @pl.when(edge)
        def _(side=side):
            def each(j, carry):
                @pl.when((j <= t) if side == 0 else (j >= t))
                def _():
                    for c in range(PARTS):
                        q_copy(j, c, side).wait_send()

                @pl.when((j > t) if side == 0 else (j < t))
                def _():
                    for c in range(PARTS):
                        p_copy(j, c, side).wait_send()

                return carry

            lax.fori_loop(0, NT, each, 0)

    def left_tensor(k, _):
        to = lax.rem(t + k, NT)
        rs_copy(to, t).wait_send()
        ag_copy(to, t).wait_send()
        return _

    lax.fori_loop(1, NT, left_tensor, 0)
    for half in range(2):
        rows_copy(half).wait_send()

    def left_group(k, _):
        hand_copy(0, lax.rem(g + k, NG), g).wait_send()
        hand_copy(1, lax.rem(g + k, NG), g).wait_send()
        return _

    lax.fori_loop(1, NG, left_group, 0)
    for n in range(TOK // TILE):
        out_copy(n).wait()
    last.wait()


def body(*args):
    args = list(args)
    args[7], args[8] = args[7].T, args[8].T
    hbm = pl.BlockSpec(memory_space=pltpu.HBM)
    dma = pltpu.SemaphoreType.DMA
    return pl.pallas_call(
        kernel,
        out_shape=(
            jax.ShapeDtypeStruct((TOK, GQA * HEAD), BF16),
            jax.ShapeDtypeStruct((REQ * SPEC, GQA * HEAD), BF16),
        ),
        in_specs=[hbm] * 12,
        out_specs=(hbm, hbm),
        scratch_shapes=[
            pltpu.VMEM((TOK, NT * HEAD), BF16),
            pltpu.VMEM((TOK, GQA * HEAD), BF16),
            pltpu.VMEM((TOK, KVW), BF16),
            pltpu.VMEM((ADAPTERS, NT * HEAD, HEAD), BF16),
            pltpu.VMEM((ADAPTERS, HEAD, KVW), BF16),
            pltpu.VMEM((REQ, 32, NT * KVW), BF16),
            pltpu.VMEM((REQ * SPEC, KVW), BF16),
            pltpu.VMEM((NT, REQ * SPEC, GQA * HEAD), BF16),
            pltpu.VMEM((NT, PARTS, HEAD, 128), F32),
            pltpu.VMEM((NT, PARTS, 8, 128), F32),
            pltpu.VMEM((NT, MSG, 128), BF16),
            pltpu.VMEM((NT, MSG, 128), BF16),
            pltpu.VMEM((NT, MSG, 128), BF16),
            pltpu.VMEM((NT, BLK, HEAD), F32),
            pltpu.VMEM((NG * MAXLEN, TOK), BF16),
            pltpu.VMEM((NT, BLK, HEAD), BF16),
            pltpu.VMEM((NT, BLK, HEAD), BF16),
            pltpu.VMEM((NT, BLK, HEAD), BF16),
            pltpu.VMEM((2, TOK, HEAD), BF16),
            pltpu.VMEM((2, TOK, HEAD), BF16),
            pltpu.VMEM((2, NG, MAXLEN, HEAD), BF16),
            pltpu.VMEM((2, NG, MAXLEN, HEAD), BF16),
            pltpu.VMEM((PARTS, HEAD, 128), F32),
            pltpu.VMEM((PARTS, 8, 128), F32),
            pltpu.VMEM((TOK, GQA * HEAD), BF16),
            pltpu.VMEM((REQ * SPEC, GQA * HEAD), BF16),
            pltpu.SMEM((2, REQ), jnp.int32),
            pltpu.SMEM((ADAPTERS,), jnp.int32),
            pltpu.SMEM((1, REQ), jnp.int32),
            pltpu.SMEM((REQ, 2 * NG), jnp.int32),
            pltpu.SMEM((REQ, 2 * NG), jnp.int32),
            dma((12,)),
            dma((2, NT, PARTS)),
            dma((NT, PARTS)),
            dma((2, NT, PARTS)),
            dma((2, NT, PARTS)),
            dma((NT,)),
            dma((NT,)),
            dma((NT,)),
            dma((NT,)),
            dma((2,)),
            dma((2,)),
            dma((2, NG)),
            dma((2, NG)),
            dma((TOK // TILE + 1,)),
        ],
        compiler_params=pltpu.CompilerParams(
            collective_id=0, has_side_effects=True, vmem_limit_bytes=60 << 20
        ),
    )(*args)


def solution(mesh):
    rows = ("segment", "group")
    return jax.shard_map(
        body,
        mesh=mesh,
        in_specs=(
            P(rows, "tensor"),
            P(rows, "tensor"),
            P(rows, "tensor"),
            P(None, "tensor", None),
            P(None, None, "tensor"),
            P(),
            P(rows, None),
            P(),
            P(),
            P(rows, "tensor", None),
            P(rows, "tensor"),
            P(rows, "tensor"),
        ),
        out_specs=(P(rows, "tensor"), P(rows, "tensor")),
        check_vma=False,
    )
```

time: 126 us -> 96.9 us (0.77)
  Pallas kernels: 112 us -> 91.6 us
  local copies, waits for them, and re-layouts: 12.9 us -> 3.63 us
    pallas_call x1, Pallas kernels: 112 us -> 91.6 us  [body(): pl.pallas_call(kernel, out_shape=(jax.ShapeDtypeStruct((TOK, GQA * HEAD),...]
    unnamed x24 -> x2, local copies, waits for them, and re-layouts: 12.9 us -> 3.63 us
where the time goes in v2:
time: 96.9 us; the launch traced here: 95.9 us
  Pallas kernels  91.6 us (95%)
  local copies, waits for them, and re-layouts  3.63 us (4%)
    pallas_call x1, Pallas kernels, body(): pl.pallas_call(kernel, out_shape=(jax.ShapeDtypeStruct((TOK, GQA * HEAD),...  91.6 us
    unnamed x2, local copies, waits for them, and re-layouts  3.63 us

profile of v2, /device:TPU:6, one launch (start us, length us, event | category | flops | bytes accessed | tf_op | source)
XLA Modules:
  0.0 95.9 jit_solution(447894726419460433)
XLA Ops:
  0.6 91.6 %shard_map.131 = (bf16[384,1024]{1,0:T(8,128)(2,1)}, bf16[64,1024]{1,0:T(8,128)(2,1)}) custom-call(bf16[384,1024]{1,0:T(8,128)(2,1)} %hid.1, bf16[384,1024]{1,0:T(8,128)(2,1)} %pq.1, bf16[384,256]{1,0:T(8,128)(2,1)} %pkv.1, bf16[3,1024,128]{2,1,0:T(8,128)(2,1)} %down.1, bf16[3,128,256]{2,1,0:T(8,128)(2,1)} %up.1, s32[3]{0:T(128)} %ranks_h.1, ...), custom_call_target="tpu_custom_call" | custom-call | tf_op jit(solution)/shard_map/pallas_call | solution.py:591
  92.3 2.1 %copy.16 = bf16[384,1024]{1,0:T(8,128)(2,1)} copy(bf16[384,1024]{1,0:T(8,128)(2,1)} %get-tuple-element.4) | data formatting | bytes 1572864
  94.3 1.6 %copy.17 = bf16[64,1024]{1,0:T(8,128)(2,1)} copy(bf16[64,1024]{1,0:T(8,128)(2,1)} %get-tuple-element.5) | data formatting | bytes 262144

commit v3 on v2

--- a/solution.py
+++ b/solution.py
@@ -16,9 +16,11 @@
 BLK = TOK // NT
 ADAPTERS = 3
 PARTS = 4
+HALF = NT // 2
 QROWS = REQ * SPEC // PARTS
 KVW = 2 * HEAD
 STATS = 16
+STEPS = 11
 MSG = STATS + PARTS * HEAD
 TILE = 96
 SCALE = HEAD**-0.5
@@ -26,7 +28,7 @@
 OWN_AT = 5
 HAND_AT = (9, 10)
 TILE_AT = (6, 7, 8, 9)
-HANDED_AT = 12
+HANDED_AT = 11
 NEG = -1e30
 MESH = pl.DeviceIdType.MESH
 F32 = jnp.float32
@@ -103,6 +105,8 @@
     s = lax.axis_index("segment")
     g = lax.axis_index("group")
     t = lax.axis_index("tensor")
+    low = t // HALF * HALF
+    place = t - low
 
     loads = []
     for k, (src, dst) in enumerate(
@@ -129,6 +133,89 @@
     pl.semaphore_signal(barrier, inc=1, device_id={"segment": 1 - s}, device_id_type=MESH)
     lax.fori_loop(1, NG, greet_group, 0)
 
+    def q_copy(j, c, side):
+        rows = pl.ds(c * QROWS, QROWS)
+        return pltpu.make_async_remote_copy(
+            src_ref=qall.at[j, rows],
+            dst_ref=qall.at[j, rows],
+            send_sem=qs.at[side, j, c],
+            recv_sem=qr.at[j, c],
+            device_id={"tensor": lax.rem(t + (1 if side == 0 else NT - 1), NT)},
+            device_id_type=MESH,
+        )
+
+    def part_copy(j, c, side, slot, to):
+        rows = pl.ds(0, STATS + HEAD) if c == 0 else pl.ds(STATS + c * HEAD, HEAD)
+        return pltpu.make_async_remote_copy(
+            src_ref=sendb.at[j, rows],
+            dst_ref=(recv_r if side == 0 else recv_l).at[slot, rows],
+            send_sem=ps.at[side, j, c],
+            recv_sem=pr.at[side, slot, c],
+            device_id={"tensor": to},
+            device_id_type=MESH,
+        )
+
+    def p_copy(j, c, side):
+        jump = t == (HALF - 1 if side == 0 else HALF)
+        near = lax.rem(t + (1 if side == 0 else NT - 1), NT)
+        return part_copy(j, c, side, jnp.where(jump, NT, j), jnp.where(jump, j, near))
+
+    def p_arrived(j, c, side, slot):
+        part_copy(j, c, side, slot, lax.rem(t + 1, NT)).wait_recv()
+
+    def rs_copy(k, src):
+        return pltpu.make_async_remote_copy(
+            src_ref=rs_send.at[k],
+            dst_ref=rs_recv.at[src],
+            send_sem=rss.at[k],
+            recv_sem=rsr.at[src],
+            device_id={"tensor": k},
+            device_id_type=MESH,
+        )
+
+    def ag_copy(k, src):
+        return pltpu.make_async_remote_copy(
+            src_ref=sh_own.at[src],
+            dst_ref=sh_own.at[src],
+            send_sem=ags.at[k],
+            recv_sem=agr.at[src],
+            device_id={"tensor": k},
+            device_id_type=MESH,
+        )
+
+    def rows_copy(half):
+        return pltpu.make_async_remote_copy(
+            src_ref=kv_own.at[half],
+            dst_ref=kv_oth.at[half],
+            send_sem=xs.at[half],
+            recv_sem=xr.at[half],
+            device_id={"segment": 1 - s},
+            device_id_type=MESH,
+        )
+
+    def hand_copy(half, d, src):
+        return pltpu.make_async_remote_copy(
+            src_ref=packed.at[half, d],
+            dst_ref=handed.at[half, src],
+            send_sem=hs.at[half, d],
+            recv_sem=hr.at[half, src],
+            device_id={"group": d},
+            device_id_type=MESH,
+        )
+
+    ld_q.wait()
+    pl.semaphore_wait(barrier, (NT - 1) + 1 + (NG - 1))
+
+    @pl.when(t < NT - 1)
+    def _():
+        for c in range(PARTS):
+            q_copy(t, c, 0).start()
+
+    @pl.when(t > 0)
+    def _():
+        for c in range(PARTS):
+            q_copy(t, c, 1).start()
+
     for c in loads[:4]:
         c.wait()
 
@@ -152,86 +239,11 @@
     mine[...] = selected.reshape(NT, BLK, HEAD)
     rs_send[...] = mine[...].astype(BF16)
 
-    pl.semaphore_wait(barrier, (NT - 1) + 1 + (NG - 1))
-
-    def q_copy(j, c, side):
-        rows = pl.ds(c * QROWS, QROWS)
-        return pltpu.make_async_remote_copy(
-            src_ref=qall.at[j, rows],
-            dst_ref=qall.at[j, rows],
-            send_sem=qs.at[side, j, c],
-            recv_sem=qr.at[j, c],
-            device_id={"tensor": lax.rem(t + (1 if side == 0 else NT - 1), NT)},
-            device_id_type=MESH,
-        )
-
-    def p_copy(j, c, side):
-        rows = pl.ds(0, STATS + HEAD) if c == 0 else pl.ds(STATS + c * HEAD, HEAD)
-        return pltpu.make_async_remote_copy(
-            src_ref=sendb.at[j, rows],
-            dst_ref=(recv_r if side == 0 else recv_l).at[j, rows],
-            send_sem=ps.at[side, j, c],
-            recv_sem=pr.at[side, j, c],
-            device_id={"tensor": lax.rem(t + (1 if side == 0 else NT - 1), NT)},
-            device_id_type=MESH,
-        )
-
-    def rs_copy(k, src):
-        return pltpu.make_async_remote_copy(
-            src_ref=rs_send.at[k],
-            dst_ref=rs_recv.at[src],
-            send_sem=rss.at[k],
-            recv_sem=rsr.at[src],
-            device_id={"tensor": k},
-            device_id_type=MESH,
-        )
-
-    def ag_copy(k, src):
-        return pltpu.make_async_remote_copy(
-            src_ref=sh_own.at[src],
-            dst_ref=sh_own.at[src],
-            send_sem=ags.at[k],
-            recv_sem=agr.at[src],
-            device_id={"tensor": k},
-            device_id_type=MESH,
-        )
-
-    def rows_copy(half):
-        return pltpu.make_async_remote_copy(
-            src_ref=kv_own.at[half],
-            dst_ref=kv_oth.at[half],
-            send_sem=xs.at[half],
-            recv_sem=xr.at[half],
-            device_id={"segment": 1 - s},
-            device_id_type=MESH,
-        )
-
-    def hand_copy(half, d, src):
-        return pltpu.make_async_remote_copy(
-            src_ref=packed.at[half, d],
-            dst_ref=handed.at[half, src],
-            send_sem=hs.at[half, d],
-            recv_sem=hr.at[half, src],
-            device_id={"group": d},
-            device_id_type=MESH,
-        )
-
     def rs_start(k, _):
         rs_copy(lax.rem(t + k, NT), t).start()
         return _
 
     lax.fori_loop(1, NT, rs_start, 0)
-    ld_q.wait()
-
-    @pl.when(t < NT - 1)
-    def _():
-        for c in range(PARTS):
-            q_copy(t, c, 0).start()
-
-    @pl.when(t > 0)
-    def _():
-        for c in range(PARTS):
-            q_copy(t, c, 1).start()
 
     def reduce_and_share():
         def add(k, total):
@@ -291,11 +303,11 @@
             rows_copy(half).start()
 
     def prompt_tile(n):
-        low = max(n * TILE - 32, 0)
-        keys = kv_own[0, low:low + 128]
-        values = kv_own[1, low:low + 128]
+        first_key = max(n * TILE - 32, 0)
+        keys = kv_own[0, first_key:first_key + 128]
+        values = kv_own[1, first_key:first_key + 128]
         q_pos = iota((TILE, 128), 0) + n * TILE
-        k_pos = iota((TILE, 128), 1) + low
+        k_pos = iota((TILE, 128), 1) + first_key
         first = start[n * TILE:(n + 1) * TILE].astype(jnp.int32)
         mask = (k_pos >= first) & (k_pos <= q_pos)
         rows = slice(n * TILE, (n + 1) * TILE)
@@ -365,7 +377,7 @@
 
     def next_link(j, side):
         buf = recv_r if side == 0 else recv_l
-        p_copy(j, 0, side).wait_recv()
+        p_arrived(j, 0, side, j)
         stats, factors = [], []
         for part, (m_in, total_in) in enumerate(get_stats(buf, j)):
             _, m_own, total_own = own_partial(j, part)
@@ -376,7 +388,7 @@
         put_stats(j, stats)
         for part, (f_in, f_own) in enumerate(factors):
             if part > 0:
-                p_copy(j, part, side).wait_recv()
+                p_arrived(j, part, side, j)
             put_num(j, part, get_num(buf, j, part) * f_in + own_num[j, part] * f_own)
             p_copy(j, part, side).start()
 
@@ -431,13 +443,13 @@
             )
             put_acc(part, *merge(get_acc(part), found))
 
-    def finish(side):
+    def finish(side, slot):
         buf = recv_r if side == 0 else recv_l
         for part in range(PARTS):
-            p_copy(t, part, side).wait_recv()
-        stats = get_stats(buf, t)
+            p_arrived(t, part, side, slot)
+        stats = get_stats(buf, slot)
         for part in range(PARTS):
-            put_acc(part, *merge(get_acc(part), (get_num(buf, t, part), *stats[part])))
+            put_acc(part, *merge(get_acc(part), (get_num(buf, slot, part), *stats[part])))
 
     def step(tau, carry):
         from_right = t + tau
@@ -465,7 +477,7 @@
         def _():
             attend_head(from_right)
 
-            @pl.when(t == 0)
+            @pl.when(place == 0)
             def _():
                 first_link(from_right, 0)
 
@@ -473,19 +485,19 @@
         def _():
             attend_head(from_left)
 
-            @pl.when(t == NT - 1)
+            @pl.when(place == HALF - 1)
             def _():
                 first_link(from_left, 1)
 
-        to_right = tau - t
-
-        @pl.when((t >= 1) & (to_right > t) & (to_right < NT))
+        to_right = tau - t + 2 * low
+
+        @pl.when((place >= 1) & (to_right > t) & (to_right < NT))
         def _():
             next_link(to_right, 0)
 
-        to_left = 2 * (NT - 1) - t - tau
-
-        @pl.when((t <= NT - 2) & (to_left < t) & (to_left >= 0))
+        to_left = 2 * (low + HALF - 1) - t - tau
+
+        @pl.when((place <= HALF - 2) & (to_left < t) & (to_left >= 0))
         def _():
             next_link(to_left, 1)
 
@@ -522,15 +534,23 @@
     own_and_drafts()
     find_rows()
     find_slots()
-    lax.fori_loop(1, 2 * NT - 1, step, 0)
-
-    @pl.when(t > 0)
+    lax.fori_loop(1, STEPS + 1, step, 0)
+
+    @pl.when(place > 0)
     def _():
-        finish(0)
-
-    @pl.when(t < NT - 1)
+        finish(0, t)
+
+    @pl.when(place < HALF - 1)
     def _():
-        finish(1)
+        finish(1, t)
+
+    @pl.when(t >= HALF)
+    def _():
+        finish(0, NT)
+
+    @pl.when(t < HALF)
+    def _():
+        finish(1, NT)
 
     for part in range(PARTS):
         num, _, total = get_acc(part)
@@ -608,8 +628,8 @@
             pltpu.VMEM((NT, PARTS, HEAD, 128), F32),
             pltpu.VMEM((NT, PARTS, 8, 128), F32),
             pltpu.VMEM((NT, MSG, 128), BF16),
-            pltpu.VMEM((NT, MSG, 128), BF16),
-            pltpu.VMEM((NT, MSG, 128), BF16),
+            pltpu.VMEM((NT + 1, MSG, 128), BF16),
+            pltpu.VMEM((NT + 1, MSG, 128), BF16),
             pltpu.VMEM((NT, BLK, HEAD), F32),
             pltpu.VMEM((NG * MAXLEN, TOK), BF16),
             pltpu.VMEM((NT, BLK, HEAD), BF16),
@@ -632,7 +652,7 @@
             dma((2, NT, PARTS)),
             dma((NT, PARTS)),
             dma((2, NT, PARTS)),
-            dma((2, NT, PARTS)),
+            dma((2, NT + 1, PARTS)),
             dma((NT,)),
             dma((NT,)),
             dma((NT,)),

time: 96.9 us -> 94.9 us (0.979)
  Pallas kernels: 91.6 us -> 90.5 us
    pallas_call x1, Pallas kernels: 91.6 us -> 90.5 us  [body(): pl.pallas_call(kernel, out_shape=(jax.ShapeDtypeStruct((TOK, GQA * HEAD),...]
where the time goes in v3:
time: 94.9 us; the launch traced here: 94.8 us
  Pallas kernels  90.5 us (95%)
  local copies, waits for them, and re-layouts  3.63 us (4%)
    pallas_call x1, Pallas kernels, body(): pl.pallas_call(kernel, out_shape=(jax.ShapeDtypeStruct((TOK, GQA * HEAD),...  90.5 us
    unnamed x2, local copies, waits for them, and re-layouts  3.63 us

profile of v3, /device:TPU:6, one launch (start us, length us, event | category | flops | bytes accessed | tf_op | source)
XLA Modules:
  0.0 94.8 jit_solution(1343467327914980090)
XLA Ops:
  0.6 90.5 %shard_map.131 = (bf16[384,1024]{1,0:T(8,128)(2,1)}, bf16[64,1024]{1,0:T(8,128)(2,1)}) custom-call(bf16[384,1024]{1,0:T(8,128)(2,1)} %hid.1, bf16[384,1024]{1,0:T(8,128)(2,1)} %pq.1, bf16[384,256]{1,0:T(8,128)(2,1)} %pkv.1, bf16[3,1024,128]{2,1,0:T(8,128)(2,1)} %down.1, bf16[3,128,256]{2,1,0:T(8,128)(2,1)} %up.1, s32[3]{0:T(128)} %ranks_h.1, ...), custom_call_target="tpu_custom_call" | custom-call | tf_op jit(solution)/shard_map/pallas_call | solution.py:611
  91.1 2.1 %copy.16 = bf16[384,1024]{1,0:T(8,128)(2,1)} copy(bf16[384,1024]{1,0:T(8,128)(2,1)} %get-tuple-element.4) | data formatting | bytes 1572864
  93.2 1.6 %copy.17 = bf16[64,1024]{1,0:T(8,128)(2,1)} copy(bf16[64,1024]{1,0:T(8,128)(2,1)} %get-tuple-element.5) | data formatting | bytes 262144

commit v4 on v3

--- a/solution.py
+++ b/solution.py
@@ -25,6 +25,7 @@
 TILE = 96
 SCALE = HEAD**-0.5
 SHARE_AT = 3
+LOCAL_AT = (1, 2, 4)
 OWN_AT = 5
 HAND_AT = (9, 10)
 TILE_AT = (6, 7, 8, 9)
@@ -501,6 +502,11 @@
         def _():
             next_link(to_left, 1)
 
+        for n, work in enumerate((find_rows, own_and_drafts, find_slots)):
+            @pl.when(tau == LOCAL_AT[n])
+            def _(work=work):
+                work()
+
         @pl.when(tau == SHARE_AT)
         def _():
             reduce_and_share()
@@ -531,9 +537,6 @@
     ld_pkv.wait()
     ld_up.wait()
     ld_pq.wait()
-    own_and_drafts()
-    find_rows()
-    find_slots()
     lax.fori_loop(1, STEPS + 1, step, 0)
 
     @pl.when(place > 0)

time: 94.9 us -> 95.2 us (level)
  no operation moved by 1% of the time
where the time goes in v4:
time: 95.2 us; the launch traced here: 94.3 us
  Pallas kernels  90.1 us (95%)
  local copies, waits for them, and re-layouts  3.63 us (4%)
    pallas_call x1, Pallas kernels, body(): pl.pallas_call(kernel, out_shape=(jax.ShapeDtypeStruct((TOK, GQA * HEAD),...  90.1 us
    unnamed x2, local copies, waits for them, and re-layouts  3.63 us

profile of v4, /device:TPU:6, one launch (start us, length us, event | category | flops | bytes accessed | tf_op | source)
XLA Modules:
  0.0 94.3 jit_solution(13592404458253649056)
XLA Ops:
  0.6 90.1 %shard_map.131 = (bf16[384,1024]{1,0:T(8,128)(2,1)}, bf16[64,1024]{1,0:T(8,128)(2,1)}) custom-call(bf16[384,1024]{1,0:T(8,128)(2,1)} %hid.1, bf16[384,1024]{1,0:T(8,128)(2,1)} %pq.1, bf16[384,256]{1,0:T(8,128)(2,1)} %pkv.1, bf16[3,1024,128]{2,1,0:T(8,128)(2,1)} %down.1, bf16[3,128,256]{2,1,0:T(8,128)(2,1)} %up.1, s32[3]{0:T(128)} %ranks_h.1, ...), custom_call_target="tpu_custom_call" | custom-call | tf_op jit(solution)/shard_map/pallas_call | solution.py:614
  90.7 2.1 %copy.16 = bf16[384,1024]{1,0:T(8,128)(2,1)} copy(bf16[384,1024]{1,0:T(8,128)(2,1)} %get-tuple-element.4) | data formatting | bytes 1572864
  92.8 1.6 %copy.17 = bf16[64,1024]{1,0:T(8,128)(2,1)} copy(bf16[64,1024]{1,0:T(8,128)(2,1)} %get-tuple-element.5) | data formatting | bytes 262144
